TPU v7x, 32 devices: a whole 2x2x4 slice. The times are simulated.
32 devices in a mesh: fc: 8 (over z, core), tok: 4 (over y, x).
Axes of the slice: x: 2, y: 2, z: 4, core: 2. Of those that a mesh axis runs over, the one named last changes fastest.
Arguments:
- tokens: bfloat16 [8, 32, 128, 1024], P('fc', 'tok'), may hold values from -6 to 6
- slot_keys: bfloat16 [1024, 256], replicated, may hold values from -2 to 2
- norm_gain: float32 [1024], replicated, may hold values from 0.25 to 1.75
- slot_gain: float32 [1024], replicated, may hold values from 0.25 to 1.75
- w_in: bfloat16 [64, 1024, 512], P(('fc', 'tok')), may hold values from -0.1875 to 0.1875
- w_out: bfloat16 [64, 512, 1024], P(('fc', 'tok')), may hold values from -0.25 to 0.25
- conv_weight: float32 [7, 7, 1024], replicated, may hold values from -0.875 to 0.875
- ln_gain: float32 [1024], replicated, may hold values from 0.25 to 1.75
- proj: bfloat16 [1024, 1024], replicated, may hold values from -0.1875 to 0.1875
- layer_scale: float32 [1024], replicated, may hold values from 0.25 to 1.75
Outputs:
- fields: bfloat16 [8, 32, 128, 1024], P('fc', 'tok')
All inputs are finite; a program needn't handle non-finite values.
Results may differ from a plain program's by a relative error of at most 0.008.
The roundings to bfloat16 on the way count: a program that leaves them out, or rounds other values in their place, can miss the bound.
Values may be sent and summed in bfloat16 or wider, within the bound.
No kernel may reach another device: no remote copies, remote signals or barrier semaphores. Data moves between devices by JAX's collectives and lax.ppermute only.
A program may use at most 64 MiB of HBM per device.

v0:
```python
import jax
import jax.numpy as jnp
from jax import lax
from jax.sharding import PartitionSpec as P


def with_halo(block, sides, width):
    for axis, dim in sides:
        count = lax.axis_size(axis)
        forward = [(i, i + 1) for i in range(count - 1)]
        backward = [(target, source) for source, target in forward]
        low = lax.ppermute(
            lax.slice_in_dim(block, block.shape[dim] - width, None, axis=dim), axis, forward
        )
        high = lax.ppermute(lax.slice_in_dim(block, 0, width, axis=dim), axis, backward)
        block = jnp.concatenate([low, block, high], axis=dim)
    return block


def rms_scale(value, gain):
    return value * lax.rsqrt(jnp.mean(value * value, axis=-1, keepdims=True) + 1e-06) * gain


def local(
    tokens, slot_keys, norm_gain, slot_gain, w_in, w_out, conv_weight, ln_gain, proj, layer_scale
):
    rows = tokens.shape[1]
    cols = tokens.shape[2]
    width = tokens.shape[3]
    count_fc = lax.axis_size("fc")
    count_tok = lax.axis_size("tok")
    slot_total = slot_keys.shape[1]
    slot_dev = slot_total // (count_fc * count_tok)
    cells = tokens.reshape(rows * cols, width)
    normed = rms_scale(cells.astype(jnp.float32), norm_gain).astype(jnp.bfloat16)
    logits = jnp.dot(normed, slot_keys, preferred_element_type=jnp.float32)
    peak = lax.pmax(jnp.max(logits, axis=0), "tok")
    shifted = jnp.exp(logits - peak)
    dispatch = shifted.astype(jnp.bfloat16)
    numer = lax.dot_general(
        dispatch, cells, (((0,), (0,)), ((), ())), preferred_element_type=jnp.float32
    )
    numer = numer.reshape(count_fc, count_tok * slot_dev, width)
    numer = lax.psum_scatter(
        numer.astype(jnp.bfloat16), "tok", scatter_dimension=1, tiled=True
    ).astype(jnp.float32)
    local_in = rms_scale(numer, slot_gain).astype(jnp.bfloat16)
    slot_in = lax.all_to_all(local_in, "fc", split_axis=0, concat_axis=0, tiled=True)
    grouped = slot_in.reshape(count_fc, w_in.shape[0], slot_dev // w_in.shape[0], width)
    hidden = jax.nn.gelu(
        jnp.einsum("mesd,edf->mesf", grouped, w_in, preferred_element_type=jnp.float32)
    ).astype(jnp.bfloat16)
    expert_out = jnp.einsum(
        "mesf,efd->mesd", hidden, w_out, preferred_element_type=jnp.float32
    ).astype(jnp.bfloat16)
    expert_out = expert_out.reshape(count_fc, slot_dev, width)
    returned = lax.all_to_all(expert_out, "fc", split_axis=0, concat_axis=0, tiled=True)
    every_slot = lax.all_gather(returned, "tok", axis=1, tiled=True).reshape(slot_total, width)
    combine = jax.nn.softmax(logits, axis=-1).astype(jnp.bfloat16)
    mixed = jnp.dot(combine, every_slot, preferred_element_type=jnp.float32)
    state = (cells.astype(jnp.float32) + mixed).astype(jnp.bfloat16).reshape(rows, cols, width)
    padded = with_halo(state, (("tok", 0),), 3)
    padded = jnp.concatenate([padded[:, cols - 3 :], padded, padded[:, :3]], axis=1)
    conv = jnp.zeros((rows, cols, width), jnp.float32)
    for row_tap in range(7):
        for col_tap in range(7):
            conv = (
                conv
                + padded[row_tap : row_tap + rows, col_tap : col_tap + cols].astype(jnp.float32)
                * conv_weight[row_tap, col_tap]
            )
    center = conv - jnp.mean(conv, axis=-1, keepdims=True)
    spread = jnp.mean(center * center, axis=-1, keepdims=True)
    normal = (center * lax.rsqrt(spread + 1e-06) * ln_gain).astype(jnp.bfloat16)
    branch = jnp.dot(normal.reshape(rows * cols, width), proj, preferred_element_type=jnp.float32)
    result = state.reshape(rows * cols, width).astype(jnp.float32) + layer_scale * jax.nn.gelu(
        branch
    )
    return result.astype(jnp.bfloat16).reshape(1, rows, cols, width)


def solution(mesh):
    return jax.shard_map(
        local,
        mesh=mesh,
        in_specs=(
            P("fc", "tok", None, None),
            P(),
            P(),
            P(),
            P(("fc", "tok"), None, None),
            P(("fc", "tok"), None, None),
            P(),
            P(),
            P(),
            P(),
        ),
        out_specs=P("fc", "tok", None, None),
        check_vma=False,
    )
```

profile of v0, /device:TPU:4, one launch (start us, length us, event | category | flops | bytes accessed | tf_op | source)
XLA Modules:
  0.0 195.9 jit_solution(10661281492974501635)
XLA Ops:
  6.5 2.2 %multiply_reduce_fusion.1 = f32[8,128]{1,0:T(8,128)S(1)} fusion(bf16[1,8,128,1024]{3,2,1,0:T(8,128)(2,1)} %param.10), kind=kLoop, calls=%fused_computation.19 | loop fusion | flops 3144704 | bytes 2101248 | tf_op jit(solution)/shard_map/reduce_sum | solution.py:21
  8.8 2.6 %fusion.66 = (f32[1024]{0:T(1024)S(1)}, f32[1024,256]{0,1:T(8,128)S(1)}) fusion(bf16[1024,256]{1,0:T(8,128)(2,1)} %param.11, bf16[1024,1024]{1,0:T(8,128)(2,1)} %bitcast.107, f32[1024]{0:T(1024)} %param.12, f32[1024]{0:T(1024)S(1)} %rsqrt_bitcast_fusion), kind=kOutput, calls=%fused_computation.87 | convolution fusion | flops 541326336 | bytes 3682304 | tf_op jit(solution)/shard_map/dot_general | solution.py:36
  11.4 0.0 copy-start.5
  11.4 0.3 fusion.33
  11.7 9.0 %pmax.7 = f32[256]{0:T(256)S(1)} all-reduce(f32[256]{0:T(256)S(1)} %get-tuple-element.6), channel_id=1, replica_groups=mesh['fc'=8,'tok'=4] {'tok'}, use_global_device_ids=true, to_apply=%region_4.0 | all-reduce | flops 256 | bytes 2048 | tf_op jit(solution)/shard_map/pmax | solution.py:37
  20.6 0.2 exponential_convert_fusion
  20.8 3.1 %convolution_convert_fusion = bf16[8,32,1024]{2,1,0:T(8,128)(2,1)} fusion(bf16[8,32,1024]{2,1,0:T(8,128)(2,1)S(1)} %bitcast.116, bf16[1024,1024,1]{1,0,2:T(8,128)(2,1)} %bitcast.108), kind=kOutput, calls=%fused_computation.47 | convolution fusion | flops 537133056 | bytes 3145728 | tf_op jit(solution)/shard_map/dot_general | solution.py:40
  23.9 0.0 all-reduce.3.cloned.1.call-update
  24.0 0.7 dynamic-slice
  25.3 44.3 %all-reduce.3.cloned.1.call-done = bf16[8,32,1024]{2,1,0:T(8,128)(2,1)} async-done(((bf16[8,32,1024]{2,1,0:T(8,128)(2,1)}), bf16[8,32,1024]{2,1,0:T(8,128)(2,1)}) %all-reduce.3.cloned.1.call-update) | async-done | bytes 524304
  69.6 1.0 fusion.36
  70.6 1.0 fusion.38
  71.7 11.2 %all_to_all.10 = bf16[8,8,1024]{2,1,0:T(8,128)(2,1)S(1)} all-to-all(bf16[8,8,1024]{2,1,0:T(8,128)(2,1)S(1)} %fusion.38), channel_id=1, replica_groups=mesh['fc'=8,'tok'=4] {'fc'}, dimensions={0} | all-to-all | bytes 262144 | tf_op jit(solution)/shard_map/all_to_all | solution.py:48
  82.8 0.1 copy.14
  82.9 3.0 %fusion.27 = bf16[2,8,4,1024]{3,1,2,0:T(8,128)(2,1)S(1)} fusion(bf16[2,512,1024]{2,1,0:T(8,128)(2,1)} %param.15, bf16[8,2,4,1024]{3,0,2,1:T(8,128)(2,1)S(1)} %bitcast.114, bf16[2,1024,512]{2,1,0:T(8,128)(2,1)} %param.14), kind=kOutput, calls=%fused_computation.48 | convolution fusion | flops 134578176 | bytes 4456448 | tf_op jit(solution)/shard_map/mesf,efd->mesd/dot_general | solution.py:53
  86.0 0.1 copy.15
  86.0 9.3 %all_to_all.11 = bf16[8,8,1024]{2,1,0:T(8,128)(2,1)S(1)} all-to-all(bf16[8,8,1024]{2,1,0:T(8,128)(2,1)S(1)} %copy.15), channel_id=1, replica_groups=mesh['fc'=8,'tok'=4] {'fc'}, dimensions={0} | all-to-all | bytes 262144 | tf_op jit(solution)/shard_map/all_to_all | solution.py:57
  95.3 9.2 %all_gather.3 = bf16[8,32,1024]{2,1,0:T(8,128)(2,1)S(1)} all-gather(bf16[8,8,1024]{2,1,0:T(8,128)(2,1)S(1)} %all_to_all.11), channel_id=1, replica_groups=mesh['fc'=8,'tok'=4] {'tok'}, dimensions={1}, use_global_device_ids=true | all-gather | bytes 655360 | tf_op jit(solution)/shard_map/all_gather | solution.py:58
  104.5 2.4 %fusion.2 = bf16[1024,1024]{1,0:T(8,128)(2,1)S(1)} fusion(bf16[1024,1024]{1,0:T(8,128)(2,1)} %bitcast.109, bf16[256,1024]{1,0:T(8,128)(2,1)S(1)} %bitcast.113, f32[1024,256]{0,1:T(8,128)S(1)} %get-tuple-element.63, f32[1024]{0:T(1024)S(1)} %get-tuple-element.5, f32[1024]{0:T(1024)S(1)} %get-tuple-element.62), kind=kOutput, calls=%fused_computation.5 | convolution fusion | flops 540803072 | bytes 5775360 | tf_op jit(solution)/shard_map/dot_general | solution.py:60
  106.9 0.1 fusion.62
  107.0 3.4 %collective-permute-start.1 = (bf16[3,128,1024]{2,1,0:T(8,128)(2,1)S(1)}, bf16[3,128,1024]{2,1,0:T(8,128)(2,1)S(1)}, u32[]{:S(2)}, u32[]{:S(2)}) collective-permute-start(bf16[3,128,1024]{2,1,0:T(8,128)(2,1)S(1)} %bitcast.112), channel_id=1, source_target_pairs={{1,0},{2,1},{3,2},{5,4},{6,5},{7,6},{9,8},{10,9},{11,10},{13,12},{... | collective-permute-start | bytes 2359304 | tf_op jit(solution)/shard_map/ppermute | solution.py:15
  110.4 2.7 %collective-permute-start = (bf16[3,128,1024]{2,1,0:T(8,128)(2,1)S(1)}, bf16[3,128,1024]{2,1,0:T(8,128)(2,1)S(1)}, u32[]{:S(2)}, u32[]{:S(2)}) collective-permute-start(bf16[3,128,1024]{2,1,0:T(8,128)(2,1)S(1)} %bitcast.111), channel_id=1, source_target_pairs={{0,1},{1,2},{2,3},{4,5},{5,6},{6,7},{8,9},{9,10},{10,11},{12,13},{... | collective-permute-start | bytes 2359304 | tf_op jit(solution)/shard_map/ppermute | solution.py:12
  113.2 0.1 fusion.63
  113.2 0.1 fusion.64
  113.3 15.1 %collective-permute-done.1 = bf16[3,128,1024]{2,1,0:T(8,128)(2,1)S(1)} collective-permute-done((bf16[3,128,1024]{2,1,0:T(8,128)(2,1)S(1)}, bf16[3,128,1024]{2,1,0:T(8,128)(2,1)S(1)}, u32[]{:S(2)}, u32[]{:S(2)}) %collective-permute-start.1) | collective-permute-done | bytes 786464 | tf_op jit(solution)/shard_map/ppermute | solution.py:15
  128.4 15.2 %collective-permute-done = bf16[3,128,1024]{2,1,0:T(8,128)(2,1)S(1)} collective-permute-done((bf16[3,128,1024]{2,1,0:T(8,128)(2,1)S(1)}, bf16[3,128,1024]{2,1,0:T(8,128)(2,1)S(1)}, u32[]{:S(2)}, u32[]{:S(2)}) %collective-permute-start) | collective-permute-done | bytes 786464 | tf_op jit(solution)/shard_map/ppermute | solution.py:12
  143.6 2.3 %fusion.14 = (bf16[14,131,1024]{2,1,0:T(8,128)(2,1)S(1)}, bf16[14,131,1024]{2,1,0:T(8,128)(2,1)S(1)}) fusion(bf16[3,128,1024]{2,1,0:T(8,128)(2,1)S(1)} %collective-permute-done.1, bf16[8,128,1024]{2,1,0:T(8,128)(2,1)S(1)} %bitcast.105, bf16[3,128,1024]{2,1,0:T(8,128)(2,1)S(1)} %collective-permute-done), kind=kLoop, calls=%fused_computation.24 | loop fusion | flops 45072384 | bytes 11182080 | tf_op jit(solution)/shard_map/concatenate | solution.py:63
  145.9 37.1 %fusion.61 = (f32[8,128]{1,0:T(8,128)S(1)}, f32[8,128,1024]{2,1,0:T(8,128)S(1)}) fusion(f32[1024]{0:T(1024)S(1)} %bitcast.126, bf16[14,131,1024]{2,1,0:T(8,128)(2,1)S(1)} %get-tuple-element.10, f32[1024]{0:T(1024)S(1)} %bitcast.127, f32[1024]{0:T(1024)S(1)} %bitcast.129, f32[1024]{0:T(1024)S(1)} %bitcast.130, ...), kind=kLoop, calls=%fused_computation.82 | loop fusion | flops 160431104 | bytes 96149504 | tf_op jit(solution)/shard_map/reduce_sum | solution.py:72
  183.0 0.5 multiply_reduce_fusion
  183.6 0.1 copy-done.3
  183.7 0.6 multiply_convert_fusion
  184.3 4.8 %fusion.12 = bf16[1024,1024]{1,0:T(8,128)(2,1)} fusion(bf16[1024,1024]{1,0:T(8,128)(2,1)S(1)} %fusion.2, f32[1024]{0:T(1024)S(1)} %copy-done.4, bf16[1024,1024]{1,0:T(8,128)(2,1)S(1)} %bitcast.110, bf16[1024,1024]{1,0:T(8,128)(2,1)S(1)} %copy-done), kind=kOutput, calls=%fused_computation.15 | convolution fusion | flops 2160066560 | bytes 8392704 | tf_op jit(solution)/shard_map/dot_general | solution.py:75
  (16 shorter events, 0.1 us)
Async XLA Ops:
  6.5 177.7 %copy-start = (bf16[1024,1024]{1,0:T(8,128)(2,1)S(1)}, bf16[1024,1024]{1,0:T(8,128)(2,1)}, u32[]{:S(2)}) copy-start(bf16[1024,1024]{1,0:T(8,128)(2,1)} %param.18) | copy-start | bytes 6291460
  6.5 63.1 %all-reduce.3.cloned.1.call-start = ((), (), s32[]{:S(2)}) async-start(), calls=%async_computation.2 | async-start | bytes 1048576
  11.4 12.6 %copy-start.5 = (u32[32]{0:T(128)S(1)}, u32[32]{0:T(128)}, u32[]{:S(2)}) copy-start(u32[32]{0:T(128)} %constant.34) | copy-start | bytes 388
  11.4 59.2 %copy-start.2 = (f32[1024]{0:T(1024)S(1)}, f32[1024]{0:T(1024)}, u32[]{:S(2)}) copy-start(f32[1024]{0:T(1024)} %param.13) | copy-start | bytes 12292
  104.5 8.6 %copy-start.1 = (f32[7,7,1024]{2,1,0:T(8,128)S(1)}, f32[7,7,1024]{2,1,0:T(8,128)}, u32[]{:S(2)}) copy-start(f32[7,7,1024]{2,1,0:T(8,128)} %param.16) | copy-start | bytes 602116
  107.0 21.4 %collective-permute-start.1 = (bf16[3,128,1024]{2,1,0:T(8,128)(2,1)S(1)}, bf16[3,128,1024]{2,1,0:T(8,128)(2,1)S(1)}, u32[]{:S(2)}, u32[]{:S(2)}) collective-permute-start(bf16[3,128,1024]{2,1,0:T(8,128)(2,1)S(1)} %bitcast.112), channel_id=1, source_target_pairs={{1,0},{2,1},{3,2},{5,4},{6,5},{7,6},{9,8},{10,9},{11,10},{13,12},{... | collective-permute-start | bytes 2359304 | tf_op jit(solution)/shard_map/ppermute | solution.py:15
  110.4 33.2 %collective-permute-start = (bf16[3,128,1024]{2,1,0:T(8,128)(2,1)S(1)}, bf16[3,128,1024]{2,1,0:T(8,128)(2,1)S(1)}, u32[]{:S(2)}, u32[]{:S(2)}) collective-permute-start(bf16[3,128,1024]{2,1,0:T(8,128)(2,1)S(1)} %bitcast.111), channel_id=1, source_target_pairs={{0,1},{1,2},{2,3},{4,5},{5,6},{6,7},{8,9},{9,10},{10,11},{12,13},{... | collective-permute-start | bytes 2359304 | tf_op jit(solution)/shard_map/ppermute | solution.py:12
  183.0 0.7 copy-start.3
  183.6 0.7 copy-start.4
Sparse Core Ops, SparseCore 0:
  24.1 45.4 all-reduce.2
where the time goes:
time: 196 us
  waiting for transfers between devices  74.6 us (38%)
  other arithmetic  45.2 us (23%)
  blocking collectives  38.6 us (20%)
  matrix products  15.9 us (8%)
  between operations  14.3 us (7%)
  starting transfers between devices  6.07 us (3%)
    unnamed x2, waiting for transfers between devices  44.3 us
    reduce_sum x1, other arithmetic, local(): center = conv - jnp.mean(conv, axis=-1, keepdims=True)  37.1 us
    ppermute x1, waiting for transfers between devices, with_halo(): lax.ppermute(lax.slice_in_dim(block, block.shape[dim] - width, None, axis...  15.2 us
    ppermute x1, waiting for transfers between devices, with_halo(): lax.ppermute(lax.slice_in_dim(block, 0, width, axis=dim), axis, backward)  15.1 us
    all_to_all x1, blocking collectives, local(): lax.all_to_all(local_in, 'fc', split_axis=0, concat_axis=0, tiled=True)  11.2 us
    all_to_all x1, blocking collectives, local(): lax.all_to_all(expert_out, 'fc', split_axis=0, concat_axis=0, tiled=True)  9.27 us
    all_gather x1, blocking collectives, local(): lax.all_gather(returned, 'tok', axis=1, tiled=True)  9.19 us
    pmax x1, blocking collectives, local(): peak = lax.pmax(jnp.max(logits, axis=0), 'tok')  8.95 us
  transfers between devices with their start and end apart: 3, of which 3 were waited for; matrix products, arithmetic and copies ran while one was open for 0% of the time, Pallas kernels for 0%

commit v1 on v0

--- a/solution.py
+++ b/solution.py
@@ -2,6 +2,24 @@
 import jax.numpy as jnp
 from jax import lax
 from jax.sharding import PartitionSpec as P
+
+
+def clear_set(patch, pos_dim, x_part):
+    formed = patch.shape
+    w2 = patch.reshape(*formed[:pos_dim], x_part, formed[pos_dim] // x_part, *formed[pos_dim + 1 :])
+    before = jnp.moveaxis(w2, pos_dim, 0)
+    return before
+
+
+def assign_sections(unit, dimension_no):
+    unit = jnp.moveaxis(unit, 0, dimension_no)
+    m_next = unit.shape
+    block_last = unit.reshape(
+        *m_next[:dimension_no],
+        m_next[dimension_no] * m_next[dimension_no + 1],
+        *m_next[dimension_no + 2 :]
+    )
+    return block_last
 
 
 def with_halo(block, sides, width):
@@ -24,6 +42,24 @@
 def local(
     tokens, slot_keys, norm_gain, slot_gain, w_in, w_out, conv_weight, ln_gain, proj, layer_scale
 ):
+
+    def create_islands_now(local_values, lane_axis, vals, point):
+        val = lax.axis_size(lane_axis)
+        f_next = lax.axis_index(lane_axis)
+        placed, item_now = (val, f_next)
+        part_now = clear_set(local_values, vals, placed)
+        trail = [part_now[item_now]]
+        for s in tuple(range(1, placed)):
+            a_now = part_now[item_now ^ s]
+            all_rows = lax.ppermute(
+                a_now, axis_name=lane_axis, perm=[(tick, tick ^ s) for tick in range(placed)]
+            )
+            trail.append(all_rows)
+        block_now = jnp.stack(trail)
+        part_now = block_now[item_now ^ jnp.arange(placed)]
+        taken_in = assign_sections(part_now, point)
+        return taken_in
+
     rows = tokens.shape[1]
     cols = tokens.shape[2]
     width = tokens.shape[3]
@@ -45,7 +81,7 @@
         numer.astype(jnp.bfloat16), "tok", scatter_dimension=1, tiled=True
     ).astype(jnp.float32)
     local_in = rms_scale(numer, slot_gain).astype(jnp.bfloat16)
-    slot_in = lax.all_to_all(local_in, "fc", split_axis=0, concat_axis=0, tiled=True)
+    slot_in = create_islands_now(local_in, "fc", 0, 0)
     grouped = slot_in.reshape(count_fc, w_in.shape[0], slot_dev // w_in.shape[0], width)
     hidden = jax.nn.gelu(
         jnp.einsum("mesd,edf->mesf", grouped, w_in, preferred_element_type=jnp.float32)

time: 196 us -> 201 us (1.026)
  blocking collectives: 38.6 us -> 29.3 us
  starting transfers between devices: 6.07 us -> 14.1 us
  waiting for transfers between devices: 74.6 us -> 80 us
    all_to_all x1 -> x0, blocking collectives: 11.2 us -> none  [local(): lax.all_to_all(local_in, 'fc', split_axis=0, concat_axis=0, tiled=True)]
    ppermute x0 -> x7, starting transfers between devices: none -> 8.06 us  [create_islands_now(): lax.ppermute(a_now, axis_name=lane_axis, perm=[(tick, tick ^ s) for tick...]
    ppermute x0 -> x7, waiting for transfers between devices: none -> 5.21 us  [create_islands_now(): lax.ppermute(a_now, axis_name=lane_axis, perm=[(tick, tick ^ s) for tick...]
  transfers between devices with their start and end apart: 3 -> 10, of which waited for: 3 -> 5; matrix products, arithmetic and copies ran while one was open for 0% -> 0% of each run, Pallas kernels for 0% -> 0%
where the time goes in v1:
time: 201 us
  waiting for transfers between devices  80 us (40%)
  other arithmetic  45.2 us (22%)
  blocking collectives  29.3 us (15%)
  matrix products  15.9 us (8%)
  between operations  14.3 us (7%)
  starting transfers between devices  14.1 us (7%)
    unnamed x2, waiting for transfers between devices  44.4 us
    reduce_sum x1, other arithmetic, local(): center = conv - jnp.mean(conv, axis=-1, keepdims=True)  37.1 us
    ppermute x1, waiting for transfers between devices, with_halo(): lax.ppermute(lax.slice_in_dim(block, block.shape[dim] - width, None, axis...  15.2 us
    ppermute x1, waiting for transfers between devices, with_halo(): lax.ppermute(lax.slice_in_dim(block, 0, width, axis=dim), axis, backward)  15.1 us
    all_to_all x1, blocking collectives, local(): lax.all_to_all(expert_out, 'fc', split_axis=0, concat_axis=0, tiled=True)  11.2 us
    all_gather x1, blocking collectives, local(): lax.all_gather(returned, 'tok', axis=1, tiled=True)  9.19 us
    pmax x1, blocking collectives, local(): peak = lax.pmax(jnp.max(logits, axis=0), 'tok')  8.95 us
    ppermute x7, starting transfers between devices, create_islands_now(): lax.ppermute(a_now, axis_name=lane_axis, perm=[(tick, tick ^ s) for tick...  8.06 us
  transfers between devices with their start and end apart: 10, of which 5 were waited for; matrix products, arithmetic and copies ran while one was open for 0% of the time, Pallas kernels for 0%

profile of v1, /device:TPU:4, one launch (start us, length us, event | category | flops | bytes accessed | tf_op | source)
XLA Modules:
  0.0 200.6 jit_solution(16844146886905436051)
XLA Ops:
  6.5 2.2 %multiply_reduce_fusion.1 = f32[8,128]{1,0:T(8,128)S(1)} fusion(bf16[1,8,128,1024]{3,2,1,0:T(8,128)(2,1)} %param.10), kind=kLoop, calls=%fused_computation.20 | loop fusion | flops 3144704 | bytes 2101248 | tf_op jit(solution)/shard_map/reduce_sum | solution.py:39
  8.8 2.6 %fusion.67 = (f32[1024]{0:T(1024)S(1)}, f32[1024,256]{0,1:T(8,128)S(1)}) fusion(bf16[1024,256]{1,0:T(8,128)(2,1)} %param.11, bf16[1024,1024]{1,0:T(8,128)(2,1)} %bitcast.126, f32[1024]{0:T(1024)} %param.12, f32[1024]{0:T(1024)S(1)} %rsqrt_bitcast_fusion), kind=kOutput, calls=%fused_computation.106 | convolution fusion | flops 541326336 | bytes 3682304 | tf_op jit(solution)/shard_map/dot_general | solution.py:72
  11.4 0.3 fusion.33
  11.7 9.0 %pmax.7 = f32[256]{0:T(256)S(1)} all-reduce(f32[256]{0:T(256)S(1)} %get-tuple-element.6), channel_id=1, replica_groups=mesh['fc'=8,'tok'=4] {'tok'}, use_global_device_ids=true, to_apply=%region_4.0 | all-reduce | flops 256 | bytes 2048 | tf_op jit(solution)/shard_map/pmax | solution.py:73
  20.6 0.2 exponential_convert_fusion
  20.9 3.1 %convolution_convert_fusion = bf16[8,32,1024]{2,1,0:T(8,128)(2,1)} fusion(bf16[8,32,1024]{2,1,0:T(8,128)(2,1)S(1)} %bitcast.135, bf16[1024,1024,1]{1,0,2:T(8,128)(2,1)} %bitcast.127), kind=kOutput, calls=%fused_computation.48 | convolution fusion | flops 537133056 | bytes 3145728 | tf_op jit(solution)/shard_map/dot_general | solution.py:76
  24.0 0.6 dynamic-slice.11
  25.2 44.4 %all-reduce.3.cloned.1.call-done = bf16[8,32,1024]{2,1,0:T(8,128)(2,1)} async-done(((bf16[8,32,1024]{2,1,0:T(8,128)(2,1)}), bf16[8,32,1024]{2,1,0:T(8,128)(2,1)}) %all-reduce.3.cloned.1.call-update) | async-done | bytes 524304
  69.6 1.0 fusion.36
  70.7 1.0 fusion.38
  71.8 3.4 %collective-permute-start.6 = (bf16[1,8,1024]{2,1,0:T(8,128)(2,1)S(1)}, bf16[1,8,1024]{2,1,0:T(8,128)(2,1)S(1)}, u32[]{:S(2)}, u32[]{:S(2)}) collective-permute-start(bf16[1,8,1024]{2,1,0:T(8,128)(2,1)S(1)} %get-tuple-element.62), channel_id=1, source_target_pairs={{0,28},{4,24},{8,20},{12,16},{16,12},{20,8},{24,4},{28,0},{1,29},{... | collective-permute-start | bytes 49160 | tf_op jit(solution)/shard_map/ppermute | solution.py:54
  75.2 0.5 collective-permute-start.5
  75.7 2.3 %collective-permute-start.3 = (bf16[1,8,1024]{2,1,0:T(8,128)(2,1)S(1)}, bf16[1,8,1024]{2,1,0:T(8,128)(2,1)S(1)}, u32[]{:S(2)}, u32[]{:S(2)}) collective-permute-start(bf16[1,8,1024]{2,1,0:T(8,128)(2,1)S(1)} %get-tuple-element.65), channel_id=1, source_target_pairs={{0,16},{4,20},{8,24},{12,28},{16,0},{20,4},{24,8},{28,12},{1,17},{... | collective-permute-start | bytes 49160 | tf_op jit(solution)/shard_map/ppermute | solution.py:54
  78.1 1.6 collective-permute-start.1
  79.7 2.1 %collective-permute-done.1 = bf16[1,8,1024]{2,1,0:T(8,128)(2,1)S(1)} collective-permute-done((bf16[1,8,1024]{2,1,0:T(8,128)(2,1)S(1)}, bf16[1,8,1024]{2,1,0:T(8,128)(2,1)S(1)}, u32[]{:S(2)}, u32[]{:S(2)}) %collective-permute-start.1) | collective-permute-done | bytes 16416 | tf_op jit(solution)/shard_map/ppermute | solution.py:54
  81.8 0.1 collective-permute-start.2
  81.9 3.1 %collective-permute-done.2 = bf16[1,8,1024]{2,1,0:T(8,128)(2,1)S(1)} collective-permute-done((bf16[1,8,1024]{2,1,0:T(8,128)(2,1)S(1)}, bf16[1,8,1024]{2,1,0:T(8,128)(2,1)S(1)}, u32[]{:S(2)}, u32[]{:S(2)}) %collective-permute-start.2) | collective-permute-done | bytes 16416 | tf_op jit(solution)/shard_map/ppermute | solution.py:54
  85.1 0.6 gather_fusion
  85.7 3.0 %fusion.27 = bf16[2,8,4,1024]{3,1,2,0:T(8,128)(2,1)S(1)} fusion(bf16[2,512,1024]{2,1,0:T(8,128)(2,1)} %param.15, bf16[8,2,4,1024]{3,0,2,1:T(8,128)(2,1)S(1)} %bitcast.133, bf16[2,1024,512]{2,1,0:T(8,128)(2,1)} %param.14), kind=kOutput, calls=%fused_computation.49 | convolution fusion | flops 134578176 | bytes 4456448 | tf_op jit(solution)/shard_map/mesf,efd->mesd/dot_general | solution.py:89
  88.8 11.2 %all_to_all.5 = bf16[8,8,1024]{2,1,0:T(8,128)(2,1)S(1)} all-to-all(bf16[8,8,1024]{2,1,0:T(8,128)(2,1)S(1)} %copy.15), channel_id=1, replica_groups=mesh['fc'=8,'tok'=4] {'fc'}, dimensions={0} | all-to-all | bytes 262144 | tf_op jit(solution)/shard_map/all_to_all | solution.py:93
  100.0 9.2 %all_gather.3 = bf16[8,32,1024]{2,1,0:T(8,128)(2,1)S(1)} all-gather(bf16[8,8,1024]{2,1,0:T(8,128)(2,1)S(1)} %all_to_all.5), channel_id=1, replica_groups=mesh['fc'=8,'tok'=4] {'tok'}, dimensions={1}, use_global_device_ids=true | all-gather | bytes 655360 | tf_op jit(solution)/shard_map/all_gather | solution.py:94
  109.2 2.4 %fusion.2 = bf16[1024,1024]{1,0:T(8,128)(2,1)S(1)} fusion(bf16[1024,1024]{1,0:T(8,128)(2,1)} %bitcast.128, bf16[256,1024]{1,0:T(8,128)(2,1)S(1)} %bitcast.132, f32[1024,256]{0,1:T(8,128)S(1)} %get-tuple-element.70, f32[1024]{0:T(1024)S(1)} %get-tuple-element.5, f32[1024]{0:T(1024)S(1)} %get-tuple-element.69), kind=kOutput, calls=%fused_computation.6 | convolution fusion | flops 540803072 | bytes 5775360 | tf_op jit(solution)/shard_map/dot_general | solution.py:96
  111.6 0.1 fusion.63
  111.7 3.4 %collective-permute-start.8 = (bf16[3,128,1024]{2,1,0:T(8,128)(2,1)S(1)}, bf16[3,128,1024]{2,1,0:T(8,128)(2,1)S(1)}, u32[]{:S(2)}, u32[]{:S(2)}) collective-permute-start(bf16[3,128,1024]{2,1,0:T(8,128)(2,1)S(1)} %bitcast.131), channel_id=1, source_target_pairs={{1,0},{2,1},{3,2},{5,4},{6,5},{7,6},{9,8},{10,9},{11,10},{13,12},{... | collective-permute-start | bytes 2359304 | tf_op jit(solution)/shard_map/ppermute | solution.py:33
  115.1 2.7 %collective-permute-start.7 = (bf16[3,128,1024]{2,1,0:T(8,128)(2,1)S(1)}, bf16[3,128,1024]{2,1,0:T(8,128)(2,1)S(1)}, u32[]{:S(2)}, u32[]{:S(2)}) collective-permute-start(bf16[3,128,1024]{2,1,0:T(8,128)(2,1)S(1)} %bitcast.130), channel_id=1, source_target_pairs={{0,1},{1,2},{2,3},{4,5},{5,6},{6,7},{8,9},{9,10},{10,11},{12,13},{... | collective-permute-start | bytes 2359304 | tf_op jit(solution)/shard_map/ppermute | solution.py:30
  118.0 15.1 %collective-permute-done.8 = bf16[3,128,1024]{2,1,0:T(8,128)(2,1)S(1)} collective-permute-done((bf16[3,128,1024]{2,1,0:T(8,128)(2,1)S(1)}, bf16[3,128,1024]{2,1,0:T(8,128)(2,1)S(1)}, u32[]{:S(2)}, u32[]{:S(2)}) %collective-permute-start.8) | collective-permute-done | bytes 786464 | tf_op jit(solution)/shard_map/ppermute | solution.py:33
  133.1 15.2 %collective-permute-done.7 = bf16[3,128,1024]{2,1,0:T(8,128)(2,1)S(1)} collective-permute-done((bf16[3,128,1024]{2,1,0:T(8,128)(2,1)S(1)}, bf16[3,128,1024]{2,1,0:T(8,128)(2,1)S(1)}, u32[]{:S(2)}, u32[]{:S(2)}) %collective-permute-start.7) | collective-permute-done | bytes 786464 | tf_op jit(solution)/shard_map/ppermute | solution.py:30
  148.3 2.3 %fusion.14 = (bf16[14,131,1024]{2,1,0:T(8,128)(2,1)S(1)}, bf16[14,131,1024]{2,1,0:T(8,128)(2,1)S(1)}) fusion(bf16[3,128,1024]{2,1,0:T(8,128)(2,1)S(1)} %collective-permute-done.8, bf16[8,128,1024]{2,1,0:T(8,128)(2,1)S(1)} %bitcast.124, bf16[3,128,1024]{2,1,0:T(8,128)(2,1)S(1)} %collective-permute-done.7), kind=kLoop, calls=%fused_computation.25 | loop fusion | flops 45072384 | bytes 11182080 | tf_op jit(solution)/shard_map/concatenate | solution.py:99
  150.6 37.1 %fusion.62 = (f32[8,128]{1,0:T(8,128)S(1)}, f32[8,128,1024]{2,1,0:T(8,128)S(1)}) fusion(f32[1024]{0:T(1024)S(1)} %bitcast.146, bf16[14,131,1024]{2,1,0:T(8,128)(2,1)S(1)} %get-tuple-element.10, f32[1024]{0:T(1024)S(1)} %bitcast.147, f32[1024]{0:T(1024)S(1)} %bitcast.149, f32[1024]{0:T(1024)S(1)} %bitcast.150, ...), kind=kLoop, calls=%fused_computation.101 | loop fusion | flops 160431104 | bytes 96149504 | tf_op jit(solution)/shard_map/reduce_sum | solution.py:108
  187.7 0.5 multiply_reduce_fusion
  188.4 0.6 multiply_convert_fusion
  189.0 4.8 %fusion.12 = bf16[1024,1024]{1,0:T(8,128)(2,1)} fusion(bf16[1024,1024]{1,0:T(8,128)(2,1)S(1)} %fusion.2, f32[1024]{0:T(1024)S(1)} %copy-done.4, bf16[1024,1024]{1,0:T(8,128)(2,1)S(1)} %bitcast.129, bf16[1024,1024]{1,0:T(8,128)(2,1)S(1)} %copy-done), kind=kOutput, calls=%fused_computation.16 | convolution fusion | flops 2160066560 | bytes 8392704 | tf_op jit(solution)/shard_map/dot_general | solution.py:111
  (41 shorter events, 0.6 us)
Async XLA Ops:
  6.5 182.4 %copy-start = (bf16[1024,1024]{1,0:T(8,128)(2,1)S(1)}, bf16[1024,1024]{1,0:T(8,128)(2,1)}, u32[]{:S(2)}) copy-start(bf16[1024,1024]{1,0:T(8,128)(2,1)} %param.18) | copy-start | bytes 6291460
  6.5 63.1 %all-reduce.3.cloned.1.call-start = ((), (), s32[]{:S(2)}) async-start(), calls=%async_computation.1 | async-start | bytes 1048576
  11.4 12.6 %copy-start.5 = (u32[32]{0:T(128)S(1)}, u32[32]{0:T(128)}, u32[]{:S(2)}) copy-start(u32[32]{0:T(128)} %constant.60) | copy-start | bytes 388
  11.4 59.2 %copy-start.2 = (f32[1024]{0:T(1024)S(1)}, f32[1024]{0:T(1024)}, u32[]{:S(2)}) copy-start(f32[1024]{0:T(1024)} %param.13) | copy-start | bytes 12292
  71.7 6.4 %collective-permute-start = (bf16[1,8,1024]{2,1,0:T(8,128)(2,1)S(1)}, bf16[1,8,1024]{2,1,0:T(8,128)(2,1)S(1)}, u32[]{:S(2)}, u32[]{:S(2)}) collective-permute-start(bf16[1,8,1024]{2,1,0:T(8,128)(2,1)S(1)} %get-tuple-element.68), channel_id=1, source_target_pairs={{0,4},{4,0},{8,12},{12,8},{16,20},{20,16},{24,28},{28,24},{1,5},{5... | collective-permute-start | bytes 49160 | tf_op jit(solution)/shard_map/ppermute | solution.py:54
  71.8 13.2 %collective-permute-start.6 = (bf16[1,8,1024]{2,1,0:T(8,128)(2,1)S(1)}, bf16[1,8,1024]{2,1,0:T(8,128)(2,1)S(1)}, u32[]{:S(2)}, u32[]{:S(2)}) collective-permute-start(bf16[1,8,1024]{2,1,0:T(8,128)(2,1)S(1)} %get-tuple-element.62), channel_id=1, source_target_pairs={{0,28},{4,24},{8,20},{12,16},{16,12},{20,8},{24,4},{28,0},{1,29},{... | collective-permute-start | bytes 49160 | tf_op jit(solution)/shard_map/ppermute | solution.py:54
  75.2 9.8 %collective-permute-start.5 = (bf16[1,8,1024]{2,1,0:T(8,128)(2,1)S(1)}, bf16[1,8,1024]{2,1,0:T(8,128)(2,1)S(1)}, u32[]{:S(2)}, u32[]{:S(2)}) collective-permute-start(bf16[1,8,1024]{2,1,0:T(8,128)(2,1)S(1)} %get-tuple-element.63), channel_id=1, source_target_pairs={{0,24},{4,28},{8,16},{12,20},{16,8},{20,12},{24,0},{28,4},{1,25},{... | collective-permute-start | bytes 49160 | tf_op jit(solution)/shard_map/ppermute | solution.py:54
  75.7 9.3 %collective-permute-start.4 = (bf16[1,8,1024]{2,1,0:T(8,128)(2,1)S(1)}, bf16[1,8,1024]{2,1,0:T(8,128)(2,1)S(1)}, u32[]{:S(2)}, u32[]{:S(2)}) collective-permute-start(bf16[1,8,1024]{2,1,0:T(8,128)(2,1)S(1)} %get-tuple-element.64), channel_id=1, source_target_pairs={{0,20},{4,16},{8,28},{12,24},{16,4},{20,0},{24,12},{28,8},{1,21},{... | collective-permute-start | bytes 49160 | tf_op jit(solution)/shard_map/ppermute | solution.py:54
  75.7 9.3 %collective-permute-start.3 = (bf16[1,8,1024]{2,1,0:T(8,128)(2,1)S(1)}, bf16[1,8,1024]{2,1,0:T(8,128)(2,1)S(1)}, u32[]{:S(2)}, u32[]{:S(2)}) collective-permute-start(bf16[1,8,1024]{2,1,0:T(8,128)(2,1)S(1)} %get-tuple-element.65), channel_id=1, source_target_pairs={{0,16},{4,20},{8,24},{12,28},{16,0},{20,4},{24,8},{28,12},{1,17},{... | collective-permute-start | bytes 49160 | tf_op jit(solution)/shard_map/ppermute | solution.py:54
  78.1 3.7 %collective-permute-start.1 = (bf16[1,8,1024]{2,1,0:T(8,128)(2,1)S(1)}, bf16[1,8,1024]{2,1,0:T(8,128)(2,1)S(1)}, u32[]{:S(2)}, u32[]{:S(2)}) collective-permute-start(bf16[1,8,1024]{2,1,0:T(8,128)(2,1)S(1)} %get-tuple-element.67), channel_id=1, source_target_pairs={{0,8},{4,12},{8,0},{12,4},{16,24},{20,28},{24,16},{28,20},{1,9},{5... | collective-permute-start | bytes 49160 | tf_op jit(solution)/shard_map/ppermute | solution.py:54
  81.8 3.2 %collective-permute-start.2 = (bf16[1,8,1024]{2,1,0:T(8,128)(2,1)S(1)}, bf16[1,8,1024]{2,1,0:T(8,128)(2,1)S(1)}, u32[]{:S(2)}, u32[]{:S(2)}) collective-permute-start(bf16[1,8,1024]{2,1,0:T(8,128)(2,1)S(1)} %get-tuple-element.66), channel_id=1, source_target_pairs={{0,12},{4,8},{8,4},{12,0},{16,28},{20,24},{24,20},{28,16},{1,13},{... | collective-permute-start | bytes 49160 | tf_op jit(solution)/shard_map/ppermute | solution.py:54
  109.2 8.6 %copy-start.1 = (f32[7,7,1024]{2,1,0:T(8,128)S(1)}, f32[7,7,1024]{2,1,0:T(8,128)}, u32[]{:S(2)}) copy-start(f32[7,7,1024]{2,1,0:T(8,128)} %param.16) | copy-start | bytes 602116
  111.7 21.4 %collective-permute-start.8 = (bf16[3,128,1024]{2,1,0:T(8,128)(2,1)S(1)}, bf16[3,128,1024]{2,1,0:T(8,128)(2,1)S(1)}, u32[]{:S(2)}, u32[]{:S(2)}) collective-permute-start(bf16[3,128,1024]{2,1,0:T(8,128)(2,1)S(1)} %bitcast.131), channel_id=1, source_target_pairs={{1,0},{2,1},{3,2},{5,4},{6,5},{7,6},{9,8},{10,9},{11,10},{13,12},{... | collective-permute-start | bytes 2359304 | tf_op jit(solution)/shard_map/ppermute | solution.py:33
  115.1 33.2 %collective-permute-start.7 = (bf16[3,128,1024]{2,1,0:T(8,128)(2,1)S(1)}, bf16[3,128,1024]{2,1,0:T(8,128)(2,1)S(1)}, u32[]{:S(2)}, u32[]{:S(2)}) collective-permute-start(bf16[3,128,1024]{2,1,0:T(8,128)(2,1)S(1)} %bitcast.130), channel_id=1, source_target_pairs={{0,1},{1,2},{2,3},{4,5},{5,6},{6,7},{8,9},{9,10},{10,11},{12,13},{... | collective-permute-start | bytes 2359304 | tf_op jit(solution)/shard_map/ppermute | solution.py:30
  187.7 0.7 copy-start.3
  188.3 0.7 copy-start.4
Sparse Core Ops, SparseCore 0:
  24.1 45.4 all-reduce.2
